TPU v7x, 256 devices: a whole 4x4x8 slice. The times are simulated.
256 devices in a mesh: tiles: 256 (over z, x, y, core).
Axes of the slice: x: 4, y: 4, z: 8, core: 2. Of those that a mesh axis runs over, the one named last changes fastest.
Arguments:
- ocean_state: bfloat16 [1024, 32, 32, 95], P('tiles'), may hold values from -6 to 6
- cotangent: bfloat16 [1024, 32, 32, 192], P('tiles'), may hold values from -6 to 6
- w_stem: bfloat16 [95, 192], replicated, may hold values from -0.625 to 0.625
- dw_kernel: bfloat16 [7, 7, 192], replicated, may hold values from -0.875 to 0.875
- norm_gain: float32 [192], replicated, may hold values from 0.25 to 1.75
- w_up: bfloat16 [192, 768], replicated, may hold values from -0.4375 to 0.4375
- w_down: bfloat16 [768, 192], replicated, may hold values from -0.21875 to 0.21875
- tile_links: int32 [1024, 4], P('tiles'), may hold values from -1 to 3, as said below
- fold_flags: int32 [1024], P('tiles'), may hold values from 0 to 1, as said below
- wet_count: int32 [256], P('tiles'), may hold values from 1 to 4, as said below
Outputs:
- grad_state: bfloat16 [1024, 32, 32, 95], P('tiles')
- grad_stem: float32 [95, 192], replicated
- grad_kernel: float32 [7, 7, 192], replicated
- grad_gain: float32 [192], replicated
- grad_up: float32 [192, 768], replicated
- grad_down: float32 [768, 192], replicated
Inputs may be any that keep to these rules, and one draw needn't show every extreme that they name: `tile_links`: each slot's west and east links name a slot of the device before and after it (wrapping), its south and north links a slot of its own device, -1 for land, outside the grid and across the fold. Links are mutual: a slot's east neighbour has it as west neighbour, its north neighbour has it as south neighbour. Empty slots have -1 in every column and no link names them. `fold_flags`: at most one slot a device is marked, a live tile of the top tile row; device d's mark equals its mirror device's mark. Live slots are slots 0 to wet_count - 1 of a device; some device is full.
All inputs are finite; a program needn't handle non-finite values.
Results may differ from a plain program's by a relative error of at most 0.0071.
Values may be sent and summed in bfloat16 or wider, within the bound.
No kernel may reach another device: no remote copies, remote signals or barrier semaphores. Data moves between devices by JAX's collectives and lax.ppermute only.
A program may use at most 128 MiB of HBM per device.

v0:
```python
import jax
import jax.numpy as jnp
from jax import lax
from jax.experimental import pallas as pl
from jax.experimental.pallas import tpu as pltpu
from jax.sharding import PartitionSpec as P


epsilon = 1e-06
root_half = 0.7071067811865476
inv_root_two_pi = 0.3989422804014327
SLOTS = 4
SIDE = 32
QROWS = 8
SUB = 16
CW = 192
CP = 256
FF = 768
EW = SIDE + 6
GW = SIDE + 12
EP = EW // 2
GP = GW // 2
GS = SIDE + 16
NFOLD = 3 * EW
bf16 = jnp.bfloat16
f32 = jnp.float32
VMEM = pl.BlockSpec(memory_space=pltpu.VMEM)
SMEM = pl.BlockSpec(memory_space=pltpu.SMEM)


def call(kernel, outs, specs, scratch=(), micros=1):
    single = not isinstance(outs, (list, tuple))
    return pl.pallas_call(
        kernel,
        out_shape=outs,
        in_specs=specs,
        out_specs=VMEM if single else [VMEM] * len(outs),
        scratch_shapes=list(scratch),
        compiler_params=pltpu.CompilerParams(vmem_limit_bytes=52 * 1024 * 1024),
        cost_estimate=pl.CostEstimate(
            flops=micros * 1_150_000_000, bytes_accessed=micros * 1_000_000, transcendentals=0
        ),
    )


def struct(shape, dtype):
    return jax.ShapeDtypeStruct(shape, dtype)


def dot(a, b):
    return jnp.dot(a, b, preferred_element_type=f32)


def dot_t(a, b):
    return lax.dot_general(a, b, (((0,), (0,)), ((), ())), preferred_element_type=f32)


def iotas():
    row = lax.broadcasted_iota(jnp.int32, (256, 256), 0)
    col = lax.broadcasted_iota(jnp.int32, (256, 256), 1)
    return row, col


def one_hot(mask):
    return jnp.where(mask, 1.0, 0.0).astype(bf16)


def swap_matrix():
    row, col = iotas()
    return one_hot(col == (row & 15) * 16 + (row >> 4))


def by_slot(slot, links_ref, column):
    link = jnp.full_like(slot, -1)
    for n in range(SLOTS):
        link = jnp.where(slot == n, links_ref[n, column], link)
    return link


def side_matrix(links_ref, column):
    row, col = iotas()
    s = row & 15
    link = by_slot(s & 3, links_ref, column)
    target = jnp.where(link >= 0, row - (s & 3) + link, -1)
    return one_hot(col == target)


def south_matrix(links_ref):
    row, col = iotas()
    s = row & 15
    link = by_slot(s & 3, links_ref, 2)
    target = jnp.where(s >= 4, row - 4, jnp.where(link >= 0, row - s + 12 + link, -1))
    return one_hot(col == target)


def north_matrix(links_ref):
    row, col = iotas()
    s = row & 15
    link = by_slot(s & 3, links_ref, 3)
    target = jnp.where(s < 12, row + 4, jnp.where(link >= 0, row - s + link, -1))
    return one_hot(col == target)


def starts(count):
    return [min(16 * n, count - 16) for n in range(-(-count // 16))]


def picked(matrix, block):
    lanes = block.shape[-1]
    return dot(matrix, block.reshape(256, lanes)).astype(bf16).reshape(16, SUB, lanes)


def fold_mask(flags_ref, shape):
    s = lax.broadcasted_iota(jnp.int32, shape, len(shape) - 2)
    mask = jnp.zeros(shape, jnp.int32)
    for n in range(SLOTS):
        mask = jnp.where(s == 12 + n, flags_ref[n], mask)
    return mask == 1


def fold_spread(flags_ref, start, step=1, parity=0):
    row = lax.broadcasted_iota(jnp.int32, (256, 128), 0)
    col = lax.broadcasted_iota(jnp.int32, (256, 128), 1)
    s = row & 15
    flag = jnp.zeros_like(s)
    for n in range(SLOTS):
        flag = jnp.where(s == 12 + n, flags_ref[n], flag)
    return one_hot((flag == 1) & (col == NFOLD - 1 - parity - step * (start + (row >> 4))))


def tap_of(a, b, flip):
    return (6 - a) * 7 + 6 - b if flip else a * 7 + b


def pair_weights(diag_ref, a, flip):
    def block(b):
        if 0 <= b <= 6:
            return diag_ref[tap_of(a, b, flip)]
        return jnp.zeros((128, 128), bf16)

    rows = [jnp.concatenate([block(m), block(m - 1)], axis=1) for m in range(8)]
    return jnp.concatenate(rows, axis=0)


def pair_term(src, bases, count, diag_ref, a, flip):
    parts = []
    for n in range(4):
        at = [src[pl.ds(base + n, count)].reshape(count * SUB, CP) for base in bases]
        parts.append(jnp.concatenate(at, axis=0))
    return dot(jnp.concatenate(parts, axis=1), pair_weights(diag_ref, a, flip))


def conv_pairs(src, base, width, count, diag_ref, flip):
    total = None
    for a in range(7):
        term = pair_term(src, [base + a * width], count, diag_ref, a, flip)
        total = term if total is None else total + term
    return total


def conv_rest(src, base, width, count, kf_ref, flip):
    total = jnp.zeros((count, 2, 8, 128), f32)
    for a in range(7):
        x = src[pl.ds(base + a * width, count + 6)].astype(f32).reshape(count + 6, 2, 8, 128)
        for b in range(7):
            total = total + x[b : b + count] * kf_ref[tap_of(a, b, flip), :, 128:]
    return total.reshape(count, SUB, 128)


def gelu_parts(hidden):
    cdf = 0.5 + 0.5 * lax.erf(hidden * root_half)
    bell = jnp.exp(-0.5 * hidden * hidden) * inv_root_two_pi
    return cdf, cdf + hidden * bell


def stem_kernel(state_ref, w_ref, stem_ref, moved_ref, first_ref, last_ref):
    swap = swap_matrix()
    w = w_ref[...]

    def visit(r, carry):
        for h in range(2):
            slabs = [
                state_ref[s & 3, (s >> 2) * QROWS + r, 16 * h : 16 * h + 16, :] for s in range(SUB)
            ]
            x = dot(swap, jnp.concatenate(slabs, axis=0)).astype(bf16)
            stem_ref[r, 16 * h : 16 * h + 16] = dot(x, w).astype(bf16).reshape(16, SUB, CP)
            x = x.reshape(16, SUB, -1)
            moved_ref[r, 16 * h : 16 * h + 16] = x
            if h == 0:
                first_ref[r] = x[:3]
            else:
                last_ref[r] = x[13:]
        return carry

    lax.fori_loop(0, QROWS, visit, 0)


def cot_kernel(cot_ref, wet_ref, out_ref):
    swap = swap_matrix()

    def visit(r, carry):
        for h in range(2):
            slabs = []
            for s in range(SUB):
                slab = cot_ref[s & 3, (s >> 2) * QROWS + r, 16 * h : 16 * h + 16, :]
                slabs.append(jnp.where((s & 3) < wet_ref[0], slab, jnp.zeros_like(slab)))
            x = jnp.concatenate(slabs, axis=0)
            out_ref[r, 16 * h : 16 * h + 16] = dot(swap, x).astype(bf16).reshape(16, SUB, CW)
        return carry

    lax.fori_loop(0, QROWS, visit, 0)


def widen_kernel(
    west_ref,
    east_ref,
    stem_ref,
    stem_w_ref,
    links_ref,
    flags_ref,
    ws_out,
    es_out,
    w_out,
    e_out,
    fold_out,
    rows,
):
    for source, column, raw, out in (
        (west_ref, 0, ws_out, w_out),
        (east_ref, 1, es_out, e_out),
    ):
        matrix = side_matrix(links_ref, column)
        for start in starts(24):
            got = picked(matrix, source[start : start + 16])
            raw[start : start + 16] = got
            got = dot(got.reshape(256, -1), stem_w_ref[...]).astype(bf16)
            out[start : start + 16] = got.reshape(16, SUB, CP)
    mask = fold_mask(flags_ref, (1, SUB, CP))
    rows[...] = jnp.zeros_like(rows)

    def chosen(block):
        return jnp.sum(jnp.where(mask, block.astype(f32), 0.0), axis=1)

    for k in range(3):
        rows[k * EW : k * EW + 3] = chosen(w_out[(5 + k) * 3 : (6 + k) * 3])
        rows[k * EW + 3 : k * EW + 35] = chosen(stem_ref[5 + k])
        rows[k * EW + 35 : k * EW + 38] = chosen(e_out[(5 + k) * 3 : (6 + k) * 3])
    fold_out[...] = rows[...].astype(bf16)


def fill_halo(ref, width, links_ref):
    south = south_matrix(links_ref)
    north = north_matrix(links_ref)
    for start in starts(3 * width):
        ref[start : start + 16] = picked(south, ref[8 * width + start : 8 * width + start + 16])
        top = 11 * width + start
        ref[top : top + 16] = picked(north, ref[3 * width + start : 3 * width + start + 16])


def front_kernel(
    stem_ref,
    w_ref,
    e_ref,
    partner_ref,
    cot_ref,
    diag_ref,
    kf_ref,
    gain_ref,
    up_ref,
    up_t_ref,
    down_t_ref,
    links_ref,
    flags_ref,
    ext0_ref,
    ext1_ref,
    gm0_ref,
    gm1_ref,
    gup_ref,
    gdown_ref,
    ggain_ref,
    back_ref,
    mixed_ref,
    chosen_ref,
    rows_ref,
):
    for r in range(QROWS):
        west, east = w_ref[3 * r : 3 * r + 3], e_ref[3 * r : 3 * r + 3]
        x = jnp.concatenate([west, stem_ref[r], east], axis=0)
        pairs = x[:, :, :128].reshape(EP, 2, SUB, 128)
        ext0_ref[(r + 3) * EP : (r + 4) * EP, :, :128] = pairs[:, 0]
        ext0_ref[(r + 3) * EP : (r + 4) * EP, :, 128:] = pairs[:, 1]
        ext1_ref[(r + 3) * EW : (r + 4) * EW] = x[:, :, 128:]
    fill_halo(ext0_ref, EP, links_ref)
    fill_halo(ext1_ref, EW, links_ref)
    partner = partner_ref[...]
    mask = fold_mask(flags_ref, (1, SUB, CP))
    for start in starts(3 * EP):
        top = 11 * EP + start
        halves = [dot(fold_spread(flags_ref, start, 2, n), partner[:, :128]) for n in range(2)]
        add = jnp.concatenate(halves, axis=1).astype(bf16).reshape(16, SUB, CP)
        ext0_ref[top : top + 16] = jnp.where(mask, add, ext0_ref[top : top + 16])
    for start in starts(NFOLD):
        top = 11 * EW + start
        add = dot(fold_spread(flags_ref, start), partner[:, 128:]).astype(bf16)
        ext1_ref[top : top + 16] = jnp.where(
            mask[:, :, :128], add.reshape(16, SUB, 128), ext1_ref[top : top + 16]
        )
    gm0_ref[...] = jnp.zeros_like(gm0_ref)
    gm1_ref[...] = jnp.zeros_like(gm1_ref)
    gup_ref[...] = jnp.zeros_like(gup_ref)
    gdown_ref[...] = jnp.zeros_like(gdown_ref)
    ggain_ref[...] = jnp.zeros_like(ggain_ref)
    chosen_ref[...] = jnp.zeros_like(chosen_ref)

    mixed_ref[:, :, :, :, :128] = jnp.zeros((QROWS, 16, 2, SUB, 128), f32)

    def mix_rest(r):
        for block in range(4):
            mixed_ref[r, 4 * block : 4 * block + 4, :, :, 128:] = conv_rest(
                ext1_ref, r * EW + 8 * block, EW, 8, kf_ref, False
            ).reshape(4, 2, SUB, 128)

    def mix(a, carry):
        for r in (0, 4):
            got = pair_term(ext0_ref, [(r + k + a) * EP for k in range(4)], 16, diag_ref, a, False)
            for n in range(2):
                half = got[:, 128 * n : 128 * n + 128].reshape(4, 16, SUB, 128)
                mixed_ref[r : r + 4, :, n, :, :128] += half
        mix_rest(a)
        return carry

    lax.fori_loop(0, 7, mix, 0)
    mix_rest(7)

    def visit(r, carry):
        mixed = mixed_ref[r].reshape(512, CP)
        lane = lax.broadcasted_iota(jnp.int32, (1, CP), 1)
        average = jnp.sum(mixed, axis=-1, keepdims=True) * (1.0 / CW)
        centred = jnp.where(lane < CW, mixed - average, 0.0)
        variance = jnp.sum(centred * centred, axis=-1, keepdims=True) * (1.0 / CW)
        inv_std = lax.rsqrt(variance + epsilon)
        normed = centred * inv_std
        gain = gain_ref[...]
        low = (normed * gain).astype(bf16)
        cot = cot_ref[r].reshape(512, CW)
        grad_normed = jnp.zeros((512, CP), f32)
        for c in range(3):
            cols = slice(256 * c, 256 * c + 256)
            hidden = dot(low, up_ref[:, cols])
            grad_act = dot(cot, down_t_ref[:, cols])
            cdf, slope = gelu_parts(hidden)
            act = (hidden * cdf).astype(bf16)
            grad_hidden = (grad_act * slope).astype(bf16)
            gdown_ref[:, cols] += dot_t(cot, act)
            gup_ref[:, cols] += dot_t(low, grad_hidden)
            grad_normed = grad_normed + dot(grad_hidden, up_t_ref[cols, :])
        product = grad_normed * normed
        ggain_ref[...] += jnp.sum(product.reshape(64, 8, CP), axis=0)
        grad_unit = grad_normed * gain
        mean_unit = jnp.sum(grad_unit, axis=-1, keepdims=True) * (1.0 / CW)
        mean_both = jnp.sum(product * gain, axis=-1, keepdims=True) * (1.0 / CW)
        grad_mixed = inv_std * (grad_unit - mean_unit - normed * mean_both)
        slots = grad_mixed.reshape(SIDE, SUB, CP)
        chosen_ref[pl.ds(r * GS + 8, SIDE)] = jnp.sum(jnp.where(mask, slots, 0.0), axis=1)
        low_mixed = slots.astype(bf16)
        pairs = low_mixed[:, :, :128].reshape(16, 2, SUB, 128)
        gm0_ref[pl.ds(r * GP + 3, 16), :, :128] = pairs[:, 0]
        gm0_ref[pl.ds(r * GP + 3, 16), :, 128:] = pairs[:, 1]
        gm1_ref[pl.ds(r * GW + 6, SIDE)] = low_mixed[:, :, 128:]
        return carry

    lax.fori_loop(0, QROWS, visit, 0)
    rows_ref[...] = jnp.zeros_like(rows_ref)
    for t in range(3):
        total = jnp.zeros((EW, CP), f32)
        for a in range(4 + t, 7):
            x = chosen_ref[(11 + t - a) * GS : (12 + t - a) * GS]
            for b in range(7):
                total = total + x[8 - b : 8 - b + EW] * kf_ref[a * 7 + b, 0:1, :]
        rows_ref[t * EW : t * EW + EW] = total
    back_ref[...] = rows_ref[...].astype(bf16)


def taps_kernel(ext0_ref, ext1_ref, gm0_ref, gm1_ref, out_ref, acc_ref, turned_ref):
    acc_ref[...] = jnp.zeros_like(acc_ref)
    for r in range(QROWS):
        g = gm0_ref[r * GP + 3 : r * GP + 19].reshape(256, CP)
        turned_ref[:, 256 * r : 256 * r + 256] = g.T
    row = lax.broadcasted_iota(jnp.int32, (128, 128), 0)
    col = lax.broadcasted_iota(jnp.int32, (128, 128), 1)
    diagonal = row == col

    def visit(a, carry):
        turned = turned_ref[...]
        sums = [jnp.zeros((8, 128), f32) for _ in range(7)]
        for n in range(4):
            at = [ext0_ref[pl.ds((r + a) * EP + n, 16)].reshape(256, CP) for r in range(QROWS)]
            both = dot(turned, jnp.concatenate(at, axis=0))
            for out_col in range(2):
                for in_col in range(2):
                    b = 2 * n + in_col - out_col
                    if 0 <= b <= 6:
                        part = both[
                            128 * out_col : 128 * out_col + 128, 128 * in_col : 128 * in_col + 128
                        ]
                        part = jnp.where(diagonal, part, 0.0).reshape(16, 8, 128)
                        sums[b] = sums[b] + jnp.sum(part, axis=0)
        for b in range(7):
            acc_ref[a * 7 + b, :, :128] += sums[b]
        rest = [jnp.zeros((2, 8, 128), f32) for _ in range(7)]
        for r in range(QROWS):
            for block in range(4):
                x = ext1_ref[pl.ds((r + a) * EW + 8 * block, 14)].astype(f32)
                g = gm1_ref[r * GW + 6 + 8 * block : r * GW + 14 + 8 * block].astype(f32)
                x = x.reshape(14, 2, 8, 128)
                g = g.reshape(8, 2, 8, 128)
                for b in range(7):
                    for n in range(8):
                        rest[b] = rest[b] + x[b + n] * g[n]
        for b in range(7):
            acc_ref[a * 7 + b, :, 128:] += rest[b][0] + rest[b][1]
        return carry

    lax.fori_loop(0, 7, visit, 0)
    out_ref[...] = jnp.sum(acc_ref[...], axis=1)


def back_kernel(
    gm0_ref,
    gm1_ref,
    diag_ref,
    kf_ref,
    partner_ref,
    cot_ref,
    moved_ref,
    ws_ref,
    es_ref,
    links_ref,
    flags_ref,
    after_ref,
    mid_ref,
    w_ref,
    e_ref,
    gstem_ref,
    gmx0,
    gmx1,
    row,
):
    for source, target, width in ((gm0_ref, gmx0, GP), (gm1_ref, gmx1, GW)):
        edge = jnp.zeros((3 * width, SUB, target.shape[-1]), bf16)
        target[0 : 3 * width] = edge
        target[3 * width : 11 * width] = source[...]
        target[11 * width : 14 * width] = edge
        fill_halo(target, width, links_ref)

    def visit(r, carry):
        pairs = conv_pairs(gmx0, r * GP, GP, EP, diag_ref, True)
        for n in range(2):
            row[r, :, n, :, :128] = pairs[:, 128 * n : 128 * n + 128].reshape(EP, SUB, 128)
        for q in range(0, EW, 8):
            count = min(8, EW - q)
            row[r, q // 2 : (q + count) // 2, :, :, 128:] = conv_rest(
                gmx1, r * GW + q, GW, count, kf_ref, True
            ).reshape(count // 2, 2, SUB, 128)
        return carry

    lax.fori_loop(0, QROWS, visit, 0)
    partner = partner_ref[...]
    for k in range(3):
        for q in (0, 16, EW - 16):
            skip = 10 if q == EW - 16 else 0
            add = dot(fold_spread(flags_ref, k * EW + q), partner).reshape(16, SUB, CP)
            row[5 + k, (q + skip) // 2 : q // 2 + 8] += add[skip:].reshape(-1, 2, SUB, CP)
    for r in range(QROWS):
        full = row[r].reshape(EW, SUB, CP)
        mid_ref[r] = full[3:35]
        w_ref[3 * r : 3 * r + 3] = full[0:3].astype(bf16)
        e_ref[3 * r : 3 * r + 3] = full[35:38].astype(bf16)
    cin = moved_ref.shape[-1]
    gstem = dot_t(ws_ref[...].reshape(24 * SUB, cin), w_ref[...].reshape(24 * SUB, CP))
    gstem += dot_t(es_ref[...].reshape(24 * SUB, cin), e_ref[...].reshape(24 * SUB, CP))
    gstem_ref[...] = gstem
    for r in range(QROWS):
        own = mid_ref[r, :, :, :CW] + cot_ref[r].astype(f32)
        own = own.astype(bf16).reshape(SIDE * SUB, CW)
        gstem_ref[:, :CW] += dot_t(moved_ref[r].reshape(SIDE * SUB, cin), own)


def final_kernel(
    mid_ref, cot_ref, w_ref, e_ref, stem_t_ref, links_ref, out_ref, gout
):
    swap = swap_matrix()
    gout[...] = mid_ref[...]
    gout[:, :, :, 0:CW] = gout[:, :, :, 0:CW] + cot_ref[...].astype(f32)
    for source, column, at in ((w_ref, 0, 0), (e_ref, 1, 29)):
        matrix = side_matrix(links_ref, column)
        for start in starts(24):
            got = dot(matrix, source[start : start + 16].reshape(256, CP)).reshape(16, SUB, CP)
            for n in range(16):
                if start == 8 and n < 8:
                    continue
                r, j = divmod(start + n, 3)
                gout[r, at + j] += got[n]
    def visit(r, carry):
        for h in range(2):
            low = gout[r, 16 * h : 16 * h + 16].astype(bf16).reshape(256, CP)
            low = dot(swap, low).astype(bf16)
            grad = dot(low, stem_t_ref[...]).astype(bf16)
            for s in range(SUB):
                out_ref[s & 3, (s >> 2) * QROWS + r, 16 * h : 16 * h + 16, :] = grad[
                    16 * s : 16 * s + 16
                ]
        return carry

    lax.fori_loop(0, QROWS, visit, 0)


def shifted(block, distance):
    count = lax.axis_size("tiles")
    return lax.ppermute(block, "tiles", [((i - distance) % count, i) for i in range(count)])


def levels():
    left, stride, out = lax.axis_size("tiles"), 1, []
    while left > 1:
        size = 2 if stride == 1 or left % 4 else 4
        out.append((stride, size))
        stride, left = stride * size, left // size
    return out


def rotated(block, level, distance):
    stride, size = level
    route = []
    for i in range(lax.axis_size("tiles")):
        place = (i // stride) % size
        route.append((i, i + ((place + distance) % size - place) * stride))
    return lax.ppermute(block, "tiles", route)


def place_in(level):
    stride, size = level
    return (lax.axis_index("tiles") // stride) % size


def tree_sum(terms):
    while len(terms) > 1:
        half = len(terms) // 2
        terms = [terms[n] + terms[n + half] for n in range(half)]
    return terms[0]


def scatter_sum(block, level):
    size = level[1]
    rows = block.shape[0] // size
    me = place_in(level)

    def piece(distance):
        return lax.dynamic_slice_in_dim(block, ((me + distance) % size) * rows, rows, 0)

    terms = [piece(0)] + [rotated(piece(n), level, n) for n in range(1, size)]
    return tree_sum([t.astype(f32) for t in terms]).astype(bf16)


def full_sum(block, level):
    terms = [block] + [rotated(block, level, n) for n in range(1, level[1])]
    return tree_sum([t.astype(f32) for t in terms])


def sum_and_gather(block, count, level):
    size = level[1]
    rows = block.shape[0] - count
    me = place_in(level)
    terms = [block] + [rotated(block, level, n) for n in range(1, size)]
    total = tree_sum([t[:count].astype(f32) for t in terms]).astype(bf16)
    out = jnp.zeros((rows * size,) + block.shape[1:], block.dtype)
    for n, term in enumerate(terms):
        out = lax.dynamic_update_slice_in_dim(out, term[count:], ((me - n) % size) * rows, 0)
    return jnp.concatenate([total, out], axis=0)


def body(
    ocean_state,
    cotangent,
    w_stem,
    dw_kernel,
    norm_gain,
    w_up,
    w_down,
    tile_links,
    fold_flags,
    wet_count,
):
    cin = ocean_state.shape[3]
    half_way = lax.axis_size("tiles") // 2
    pad = CP - CW
    stem_w = jnp.pad(w_stem, ((0, 0), (0, pad)))
    kb = jnp.pad(dw_kernel.reshape(49, 1, CW), ((0, 0), (0, 0), (0, pad)))
    kf = jnp.broadcast_to(kb.astype(f32), (49, 8, CP))
    diag = kb[:, :, :128] * jnp.eye(128, dtype=bf16)
    gain = jnp.pad(norm_gain, (0, pad))[None]
    up = jnp.pad(w_up, ((0, pad), (0, 0)))
    down_t = w_down.T

    strip = struct((QROWS, 3, SUB, cin), bf16)
    stem, moved, first, last = call(
        stem_kernel,
        [
            struct((QROWS, SIDE, SUB, CP), bf16),
            struct((QROWS, SIDE, SUB, cin), bf16),
            strip,
            strip,
        ],
        [VMEM, VMEM],
        micros=5,
    )(ocean_state, stem_w)
    from_west = shifted(last, 1).reshape(24, SUB, cin)
    from_east = shifted(first, -1).reshape(24, SUB, cin)
    cot = call(cot_kernel, struct((QROWS, SIDE, SUB, CW), bf16), [VMEM, SMEM], micros=5)(
        cotangent, wet_count
    )
    west_state, east_state, west, east, fold = call(
        widen_kernel,
        [struct((24, SUB, cin), bf16)] * 2
        + [struct((24, SUB, CP), bf16)] * 2
        + [struct((128, CP), bf16)],
        [VMEM] * 4 + [SMEM, SMEM],
        [pltpu.VMEM((128, CP), f32)],
    )(from_west, from_east, stem, stem_w, tile_links, fold_flags)
    partner = shifted(fold, half_way)
    ext0, ext1, gm0, gm1, gup, gdown, ggain, back = call(
        front_kernel,
        [
            struct((14 * EP, SUB, CP), bf16),
            struct((14 * EW, SUB, 128), bf16),
            struct((QROWS * GP, SUB, CP), bf16),
            struct((QROWS * GW, SUB, 128), bf16),
            struct((CP, FF), f32),
            struct((CW, FF), f32),
            struct((8, CP), f32),
            struct((128, CP), bf16),
        ],
        [VMEM] * 11 + [SMEM, SMEM],
        [
            pltpu.VMEM((QROWS, 16, 2, SUB, CP), f32),
            pltpu.VMEM((QROWS * GS, CP), f32),
            pltpu.VMEM((128, CP), f32),
        ],
        micros=36,
    )(stem, west, east, partner, cot, diag, kf, gain, up, up.T, down_t, tile_links, fold_flags)
    parts = [g[:CW, 256 * c : 256 * c + 256] for g in (gup, gdown) for c in range(3)]
    big = jnp.concatenate(parts, axis=0).astype(bf16)
    plan = levels()
    for level in plan[:3]:
        big = scatter_sum(big, level)
    partner_back = shifted(back, half_way)
    gkernel = call(
        taps_kernel,
        struct((49, CP), f32),
        [VMEM] * 4,
        [pltpu.VMEM((49, 8, CP), f32), pltpu.VMEM((CP, QROWS * 256), bf16)],
        micros=15,
    )(ext0, ext1, gm0, gm1)
    mid, back_w, back_e, gstem = call(
        back_kernel,
        [
            struct((QROWS, SIDE, SUB, CP), f32),
            struct((24, SUB, CP), bf16),
            struct((24, SUB, CP), bf16),
            struct((cin, CP), f32),
        ],
        [VMEM] * 9 + [SMEM, SMEM, pl.BlockSpec(memory_space=pl.ANY)],
        [
            pltpu.VMEM((14 * GP, SUB, CP), bf16),
            pltpu.VMEM((14 * GW, SUB, 128), bf16),
            pltpu.VMEM((QROWS, EP, 2, SUB, CP), f32),
        ],
        micros=20,
    )(
        gm0,
        gm1,
        diag,
        kf,
        partner_back,
        cot,
        moved,
        west_state,
        east_state,
        tile_links,
        fold_flags,
        gkernel,
    )
    back_from_west = shifted(back_e, 1)
    back_from_east = shifted(back_w, -1)
    grad_state = call(
        final_kernel,
        struct(ocean_state.shape, bf16),
        [VMEM] * 5 + [SMEM],
        [pltpu.VMEM((QROWS, SIDE, SUB, CP), f32)],
        micros=8,
    )(mid, cot, back_from_west, back_from_east, stem_w.T, tile_links)
    rest = jnp.concatenate(
        [gstem, gkernel, jnp.sum(ggain, axis=0, keepdims=True), jnp.zeros((15, CP), f32)], axis=0
    )
    count = rest.shape[0]
    pack = jnp.concatenate([rest.astype(bf16), big], axis=0)
    for level in plan[:2:-1]:
        pack = full_sum(pack, level).astype(bf16)
    for level in plan[2::-1]:
        pack = sum_and_gather(pack, count, level)
    rest = pack[:count].astype(f32)
    big = pack[count:].astype(f32).reshape(2, 3, CW, CP)
    gup = jnp.concatenate([big[0, c] for c in range(3)], axis=1)
    gdown = jnp.concatenate([big[1, c].T for c in range(3)], axis=0)
    gstem, gkernel, ggain = rest[:cin, :CW], rest[cin : cin + 49, :CW], rest[cin + 49, :CW]
    return (grad_state, gstem, gkernel.reshape(7, 7, CW), ggain, gup, gdown)


def solution(mesh):
    return jax.shard_map(
        body,
        mesh=mesh,
        in_specs=(
            P("tiles", None, None, None),
            P("tiles", None, None, None),
            P(),
            P(),
            P(),
            P(),
            P(),
            P("tiles", None),
            P("tiles"),
            P("tiles"),
        ),
        out_specs=(P("tiles", None, None, None), P(), P(), P(), P(), P()),
        check_vma=False,
    )
```

profile of v0, /device:TPU:1, one launch (start us, length us, event | category | flops | bytes accessed | tf_op | source)
XLA Modules:
  0.0 172.8 jit_solution(795314337347659143)
XLA Ops:
  1.7 6.8 %shard_map.145 = (bf16[8,32,16,256]{3,2,1,0:T(8,128)(2,1)}, bf16[8,32,16,95]{3,2,1,0:T(8,128)(2,1)S(1)}, bf16[8,3,16,95]{3,2,1,0:T(8,128)(2,1)S(1)}, bf16[8,3,16,95]{3,2,1,0:T(8,128)(2,1)S(1)}) custom-call(bf16[4,32,32,95]{3,2,1,0:T(8,128)(2,1)} %state_ref.1, bf16[95,256]{1,0:T(8,128)(2,1)S(1)} %pad.16.clone.w_ref.stem_w_ref), custom_call_target="tpu_custom_call" | custom-call | flops 5750000128 | bytes 5000000 | tf_op jit(solution)/shard_map/pallas_call | solution.py:606
  9.5 2.7 %collective-permute-start = (bf16[8,3,16,95]{3,2,1,0:T(8,128)(2,1)S(1)}, bf16[8,3,16,95]{3,2,1,0:T(8,128)(2,1)S(1)}, u32[]{:S(2)}, u32[]{:S(2)}) collective-permute-start(bf16[8,3,16,95]{3,2,1,0:T(8,128)(2,1)S(1)} %get-tuple-element.28), channel_id=1, source_target_pairs={{255,0},{0,1},{1,2},{2,3},{3,4},{4,5},{5,6},{6,7},{7,8},{8,9},{9,1... | collective-permute-start | bytes 218888 | tf_op jit(solution)/shard_map/ppermute | solution.py:520
  13.8 4.9 %shard_map.147.cot_ref = bf16[8,32,16,192]{3,2,1,0:T(8,128)(2,1)} custom-call(bf16[4,32,32,192]{3,2,1,0:T(8,128)(2,1)} %cot_ref.1, s32[1]{0:T(128)S(6)} %copy.38.wet_ref), custom_call_target="tpu_custom_call" | custom-call | flops 5750000128 | bytes 5000000 | tf_op jit(solution)/shard_map/pallas_call | solution.py:619
  20.1 2.5 %shard_map.146 = (bf16[24,16,95]{2,1,0:T(8,128)(2,1)S(1)}, bf16[24,16,95]{2,1,0:T(8,128)(2,1)S(1)}, bf16[24,16,256]{2,1,0:T(8,128)(2,1)S(1)}, bf16[24,16,256]{2,1,0:T(8,128)(2,1)S(1)}, bf16[128,256]{1,0:T(8,128)(2,1)S(1)}) custom-call(bf16[24,16,95]{2,1,0:T(8,128)(2,1)S(1)} %bitcast.36, bf16[24,16,95]{2,1,0:T(8,128)(2,1)S(1)} %bitcast.37, ...), custom_call_target="tpu_custom_call" | custom-call | flops 1150000000 | bytes 1000000 | tf_op jit(solution)/shard_map/pallas_call | solution.py:622
  22.6 6.4 %collective-permute-start.2 = (bf16[128,256]{1,0:T(8,128)(2,1)S(1)}, bf16[128,256]{1,0:T(8,128)(2,1)S(1)}, u32[]{:S(2)}, u32[]{:S(2)}) collective-permute-start(bf16[128,256]{1,0:T(8,128)(2,1)S(1)} %get-tuple-element.32), channel_id=1, source_target_pairs={{128,0},{129,1},{130,2},{131,3},{132,4},{133,5},{134,6},{135,7},{1... | collective-permute-start | bytes 196616 | tf_op jit(solution)/shard_map/ppermute | solution.py:520
  29.0 1.7 %collective-permute-done.2.partner_ref = bf16[128,256]{1,0:T(8,128)(2,1)S(1)} collective-permute-done((bf16[128,256]{1,0:T(8,128)(2,1)S(1)}, bf16[128,256]{1,0:T(8,128)(2,1)S(1)}, u32[]{:S(2)}, u32[]{:S(2)}) %collective-permute-start.2) | collective-permute-done | bytes 65568 | tf_op jit(solution)/shard_map/ppermute | solution.py:520
  30.8 34.8 %shard_map.148 = (bf16[266,16,256]{2,1,0:T(8,128)(2,1)}, bf16[532,16,128]{2,1,0:T(8,128)(2,1)}, bf16[176,16,256]{2,1,0:T(8,128)(2,1)}, bf16[352,16,128]{2,1,0:T(...) custom-call(bf16[8,32,16,256]{3,2,1,0:T(8,128)(2,1)} %get-tuple-elem, ...), custom_call_target="tpu_custom_call" | custom-call | flops 41400000512 | bytes 36000000 | tf_op jit(solution)/shard_map/pallas_call | solution.py:631
  67.0 8.4 %collective-permute-start.6 = (bf16[576,256]{1,0:T(8,128)(2,1)S(1)}, bf16[576,256]{1,0:T(8,128)(2,1)S(1)}, u32[]{:S(2)}, u32[]{:S(2)}) collective-permute-start(bf16[576,256]{1,0:T(8,128)(2,1)S(1)} %constant_dynamic-slice_fusion.6), channel_id=1, source_target_pairs={{0,1},{1,0},{2,3},{3,2},{4,5},{5,4},{6,7},{7,6},{8,9},{9,8},{10,11... | collective-permute-start | bytes 884744 | tf_op jit(solution)/shard_map/ppermute | solution.py:538
  75.4 4.1 %collective-permute-start.3 = (bf16[128,256]{1,0:T(8,128)(2,1)S(1)}, bf16[128,256]{1,0:T(8,128)(2,1)S(1)}, u32[]{:S(2)}, u32[]{:S(2)}) collective-permute-start(bf16[128,256]{1,0:T(8,128)(2,1)S(1)} %get-tuple-element.35), channel_id=1, source_target_pairs={{128,0},{129,1},{130,2},{131,3},{132,4},{133,5},{134,6},{135,7},{1... | collective-permute-start | bytes 196616 | tf_op jit(solution)/shard_map/ppermute | solution.py:520
  79.7 1.5 collective-permute-start.8
  81.2 14.6 %shard_map.149.after_ref = f32[49,256]{1,0:T(8,128)S(1)} custom-call(bf16[266,16,256]{2,1,0:T(8,128)(2,1)} %get-tuple-element.39.ext0_ref, bf16[532,16,128]{2,1,0:T(8,128)(2,1)} %get-tuple-element.40.ext1_ref, bf16[176,16,256]{2,1,0:T(8,128)(2,1)S(1)} %copy-done.4, bf16[352,16,128]{2,1,0:T(8,128)(2,1)} %get-tuple-element.34.gm1_ref), custom_call_target="tpu_custom_call" | custom-call | flops 17250000896 | bytes 15000000 | tf_op jit(solution)/shard_map/pallas_call | solution.py:657
  98.2 18.1 %shard_map.150 = (f32[8,32,16,256]{3,2,1,0:T(8,128)}, bf16[24,16,256]{2,1,0:T(8,128)(2,1)S(1)}, bf16[24,16,256]{2,1,0:T(8,128)(2,1)S(1)}, f32[95,256]{1,0:T(8,128)S(1)}) custom-call(bf16[176,16,256]{2,1,0:T(8,128)(2,1)} %get-tuple-element.33.gm0_ref, bf16[352,16,128]{2,1,0:T(8,128)(2,1)} %get-tuple-element.34.gm1_ref, ...), custom_call_target="tpu_custom_call" | custom-call | flops 23000000512 | bytes 20000000 | tf_op jit(solution)/shard_map/pallas_call | solution.py:664
  118.1 7.1 %collective-permute-done.13 = bf16[196,256]{1,0:T(8,128)(2,1)S(1)} collective-permute-done((bf16[196,256]{1,0:T(8,128)(2,1)S(1)}, bf16[196,256]{1,0:T(8,128)(2,1)S(1)}, u32[]{:S(2)}, u32[]{:S(2)}) %collective-permute-start.13) | collective-permute-done | bytes 100384 | tf_op jit(solution)/shard_map/ppermute | solution.py:538
  125.7 1.3 collective-permute-start.15
  128.8 2.5 %collective-permute-done.15 = bf16[196,256]{1,0:T(8,128)(2,1)S(1)} collective-permute-done((bf16[196,256]{1,0:T(8,128)(2,1)S(1)}, bf16[196,256]{1,0:T(8,128)(2,1)S(1)}, u32[]{:S(2)}, u32[]{:S(2)}) %collective-permute-start.15) | collective-permute-done | bytes 100384 | tf_op jit(solution)/shard_map/ppermute | solution.py:538
  131.3 2.7 %collective-permute-done.14 = bf16[196,256]{1,0:T(8,128)(2,1)S(1)} collective-permute-done((bf16[196,256]{1,0:T(8,128)(2,1)S(1)}, bf16[196,256]{1,0:T(8,128)(2,1)S(1)}, u32[]{:S(2)}, u32[]{:S(2)}) %collective-permute-start.14) | collective-permute-done | bytes 100384 | tf_op jit(solution)/shard_map/ppermute | solution.py:538
  134.1 1.7 collective-permute-start.18
  136.2 2.0 %collective-permute-start.19 = (bf16[196,256]{1,0:T(8,128)(2,1)S(1)}, bf16[196,256]{1,0:T(8,128)(2,1)S(1)}, u32[]{:S(2)}, u32[]{:S(2)}) collective-permute-start(bf16[196,256]{1,0:T(8,128)(2,1)S(1)} %add_convert_fusion.1), channel_id=1, source_target_pairs={{0,24},{1,25},{2,26},{3,27},{4,28},{5,29},{6,30},{7,31},{8,0},{9,1... | collective-permute-start | bytes 301064 | tf_op jit(solution)/shard_map/ppermute | solution.py:538
  139.1 1.7 collective-permute-done.17
  141.5 1.7 collective-permute-start.21
  143.2 1.7 collective-permute-start.20
  145.0 8.5 %collective-permute-start.4 = (bf16[24,16,256]{2,1,0:T(8,128)(2,1)S(1)}, bf16[24,16,256]{2,1,0:T(8,128)(2,1)S(1)}, u32[]{:S(2)}, u32[]{:S(2)}) collective-permute-start(bf16[24,16,256]{2,1,0:T(8,128)(2,1)S(1)} %get-tuple-element.42), channel_id=1, source_target_pairs={{255,0},{0,1},{1,2},{2,3},{3,4},{4,5},{5,6},{6,7},{7,8},{8,9},{9,1... | collective-permute-start | bytes 589832 | tf_op jit(solution)/shard_map/ppermute | solution.py:520
  153.7 6.0 %collective-permute-start.23 = (bf16[736,256]{1,0:T(8,128)(2,1)S(1)}, bf16[736,256]{1,0:T(8,128)(2,1)S(1)}, u32[]{:S(2)}, u32[]{:S(2)}) collective-permute-start(bf16[736,256]{1,0:T(8,128)(2,1)S(1)} %pad_maximum_fusion.2), channel_id=1, source_target_pairs={{0,1},{1,0},{2,3},{3,2},{4,5},{5,4},{6,7},{7,6},{8,9},{9,8},{10,11... | collective-permute-start | bytes 1130504 | tf_op jit(solution)/shard_map/ppermute | solution.py:538
  159.7 9.2 %shard_map.151 = bf16[4,32,32,95]{3,2,1,0:T(8,128)(2,1)} custom-call(f32[8,32,16,256]{3,2,1,0:T(8,128)} %get-tuple-element.41.mid_ref, bf16[8,32,16,192]{3,2,1,0:T(8,128)(2,1)} %shard_map.147.cot_ref, bf16[24,16,256]{2,1,0:T(8,128)(2,1)S(1)} %collective-permute-done.4.w_ref, bf16[24,16,256]{2,1,0:T(8,128)(2,1)S(1)} %collective-permute-done.5.e_ref, ...), custom_call_target="tpu_custom_call" | custom-call | flops 9200000000 | bytes 8000000 | tf_op jit(solution)/shard_map/pallas_call | solution.py:695
  (116 shorter events, 18.4 us)
Async XLA Ops:
  9.5 10.6 %collective-permute-start = (bf16[8,3,16,95]{3,2,1,0:T(8,128)(2,1)S(1)}, bf16[8,3,16,95]{3,2,1,0:T(8,128)(2,1)S(1)}, u32[]{:S(2)}, u32[]{:S(2)}) collective-permute-start(bf16[8,3,16,95]{3,2,1,0:T(8,128)(2,1)S(1)} %get-tuple-element.28), channel_id=1, source_target_pairs={{255,0},{0,1},{1,2},{2,3},{3,4},{4,5},{5,6},{6,7},{7,8},{8,9},{9,1... | collective-permute-start | bytes 218888 | tf_op jit(solution)/shard_map/ppermute | solution.py:520
  12.2 7.9 %collective-permute-start.1 = (bf16[8,3,16,95]{3,2,1,0:T(8,128)(2,1)S(1)}, bf16[8,3,16,95]{3,2,1,0:T(8,128)(2,1)S(1)}, u32[]{:S(2)}, u32[]{:S(2)}) collective-permute-start(bf16[8,3,16,95]{3,2,1,0:T(8,128)(2,1)S(1)} %get-tuple-element.29), channel_id=1, source_target_pairs={{1,0},{2,1},{3,2},{4,3},{5,4},{6,5},{7,6},{8,7},{9,8},{10,9},{11,1... | collective-permute-start | bytes 218888 | tf_op jit(solution)/shard_map/ppermute | solution.py:520
  22.6 8.1 %collective-permute-start.2 = (bf16[128,256]{1,0:T(8,128)(2,1)S(1)}, bf16[128,256]{1,0:T(8,128)(2,1)S(1)}, u32[]{:S(2)}, u32[]{:S(2)}) collective-permute-start(bf16[128,256]{1,0:T(8,128)(2,1)S(1)} %get-tuple-element.32), channel_id=1, source_target_pairs={{128,0},{129,1},{130,2},{131,3},{132,4},{133,5},{134,6},{135,7},{1... | collective-permute-start | bytes 196616 | tf_op jit(solution)/shard_map/ppermute | solution.py:520
  67.0 12.5 %collective-permute-start.6 = (bf16[576,256]{1,0:T(8,128)(2,1)S(1)}, bf16[576,256]{1,0:T(8,128)(2,1)S(1)}, u32[]{:S(2)}, u32[]{:S(2)}) collective-permute-start(bf16[576,256]{1,0:T(8,128)(2,1)S(1)} %constant_dynamic-slice_fusion.6), channel_id=1, source_target_pairs={{0,1},{1,0},{2,3},{3,2},{4,5},{5,4},{6,7},{7,6},{8,9},{9,8},{10,11... | collective-permute-start | bytes 884744 | tf_op jit(solution)/shard_map/ppermute | solution.py:538
  75.4 22.8 %collective-permute-start.3 = (bf16[128,256]{1,0:T(8,128)(2,1)S(1)}, bf16[128,256]{1,0:T(8,128)(2,1)S(1)}, u32[]{:S(2)}, u32[]{:S(2)}) collective-permute-start(bf16[128,256]{1,0:T(8,128)(2,1)S(1)} %get-tuple-element.35), channel_id=1, source_target_pairs={{128,0},{129,1},{130,2},{131,3},{132,4},{133,5},{134,6},{135,7},{1... | collective-permute-start | bytes 196616 | tf_op jit(solution)/shard_map/ppermute | solution.py:520
  79.6 16.2 %collective-permute-start.9 = (bf16[144,256]{1,0:T(8,128)(2,1)S(1)}, bf16[144,256]{1,0:T(8,128)(2,1)S(1)}, u32[]{:S(2)}, u32[]{:S(2)}) collective-permute-start(bf16[144,256]{1,0:T(8,128)(2,1)S(1)} %get-tuple-element.55), channel_id=1, source_target_pairs={{0,6},{1,7},{2,0},{3,1},{4,2},{5,3},{6,4},{7,5},{8,14},{9,15},{10,... | collective-permute-start | bytes 221192 | tf_op jit(solution)/shard_map/ppermute | solution.py:538
  79.7 16.1 %collective-permute-start.8 = (bf16[144,256]{1,0:T(8,128)(2,1)S(1)}, bf16[144,256]{1,0:T(8,128)(2,1)S(1)}, u32[]{:S(2)}, u32[]{:S(2)}) collective-permute-start(bf16[144,256]{1,0:T(8,128)(2,1)S(1)} %get-tuple-element.56), channel_id=1, source_target_pairs={{0,2},{1,3},{2,4},{3,5},{4,6},{5,7},{6,0},{7,1},{8,10},{9,11},{10,... | collective-permute-start | bytes 221192 | tf_op jit(solution)/shard_map/ppermute | solution.py:538
  81.2 14.7 %collective-permute-start.7 = (bf16[144,256]{1,0:T(8,128)(2,1)S(1)}, bf16[144,256]{1,0:T(8,128)(2,1)S(1)}, u32[]{:S(2)}, u32[]{:S(2)}) collective-permute-start(bf16[144,256]{1,0:T(8,128)(2,1)S(1)} %get-tuple-element.54), channel_id=1, source_target_pairs={{0,4},{1,5},{2,6},{3,7},{4,0},{5,1},{6,2},{7,3},{8,12},{9,13},{10,... | collective-permute-start | bytes 221192 | tf_op jit(solution)/shard_map/ppermute | solution.py:538
  96.0 20.4 %collective-permute-start.12 = (bf16[36,256]{1,0:T(8,128)(2,1)S(1)}, bf16[36,256]{1,0:T(8,128)(2,1)S(1)}, u32[]{:S(2)}, u32[]{:S(2)}) collective-permute-start(bf16[36,256]{1,0:T(8,128)(2,1)S(1)} %get-tuple-element.58), channel_id=1, source_target_pairs={{0,24},{1,25},{2,26},{3,27},{4,28},{5,29},{6,30},{7,31},{8,0},{9,1... | collective-permute-start | bytes 55304 | tf_op jit(solution)/shard_map/ppermute | solution.py:538
  96.9 19.5 %collective-permute-start.11 = (bf16[36,256]{1,0:T(8,128)(2,1)S(1)}, bf16[36,256]{1,0:T(8,128)(2,1)S(1)}, u32[]{:S(2)}, u32[]{:S(2)}) collective-permute-start(bf16[36,256]{1,0:T(8,128)(2,1)S(1)} %get-tuple-element.59), channel_id=1, source_target_pairs={{0,8},{1,9},{2,10},{3,11},{4,12},{5,13},{6,14},{7,15},{8,16},{9,17... | collective-permute-start | bytes 55304 | tf_op jit(solution)/shard_map/ppermute | solution.py:538
  97.5 18.9 %collective-permute-start.10 = (bf16[36,256]{1,0:T(8,128)(2,1)S(1)}, bf16[36,256]{1,0:T(8,128)(2,1)S(1)}, u32[]{:S(2)}, u32[]{:S(2)}) collective-permute-start(bf16[36,256]{1,0:T(8,128)(2,1)S(1)} %get-tuple-element.57), channel_id=1, source_target_pairs={{0,16},{1,17},{2,18},{3,19},{4,20},{5,21},{6,22},{7,23},{8,24},{9,... | collective-permute-start | bytes 55304 | tf_op jit(solution)/shard_map/ppermute | solution.py:538
  116.8 8.4 %collective-permute-start.13 = (bf16[196,256]{1,0:T(8,128)(2,1)S(1)}, bf16[196,256]{1,0:T(8,128)(2,1)S(1)}, u32[]{:S(2)}, u32[]{:S(2)}) collective-permute-start(bf16[196,256]{1,0:T(8,128)(2,1)S(1)} %concatenate.23), channel_id=1, source_target_pairs={{0,128},{1,129},{2,130},{3,131},{4,132},{5,133},{6,134},{7,135},{8... | collective-permute-start | bytes 301064 | tf_op jit(solution)/shard_map/ppermute | solution.py:538
  125.2 3.6 %collective-permute-start.16 = (bf16[196,256]{1,0:T(8,128)(2,1)S(1)}, bf16[196,256]{1,0:T(8,128)(2,1)S(1)}, u32[]{:S(2)}, u32[]{:S(2)}) collective-permute-start(bf16[196,256]{1,0:T(8,128)(2,1)S(1)} %add_convert_fusion.2), channel_id=1, source_target_pairs={{0,96},{1,97},{2,98},{3,99},{4,100},{5,101},{6,102},{7,103},{8,104... | collective-permute-start | bytes 301064 | tf_op jit(solution)/shard_map/ppermute | solution.py:538
  125.7 5.7 %collective-permute-start.15 = (bf16[196,256]{1,0:T(8,128)(2,1)S(1)}, bf16[196,256]{1,0:T(8,128)(2,1)S(1)}, u32[]{:S(2)}, u32[]{:S(2)}) collective-permute-start(bf16[196,256]{1,0:T(8,128)(2,1)S(1)} %add_convert_fusion.2), channel_id=1, source_target_pairs={{0,32},{1,33},{2,34},{3,35},{4,36},{5,37},{6,38},{7,39},{8,40},{9,... | collective-permute-start | bytes 301064 | tf_op jit(solution)/shard_map/ppermute | solution.py:538
  127.0 7.0 %collective-permute-start.14 = (bf16[196,256]{1,0:T(8,128)(2,1)S(1)}, bf16[196,256]{1,0:T(8,128)(2,1)S(1)}, u32[]{:S(2)}, u32[]{:S(2)}) collective-permute-start(bf16[196,256]{1,0:T(8,128)(2,1)S(1)} %add_convert_fusion.2), channel_id=1, source_target_pairs={{0,64},{1,65},{2,66},{3,67},{4,68},{5,69},{6,70},{7,71},{8,72},{9,... | collective-permute-start | bytes 301064 | tf_op jit(solution)/shard_map/ppermute | solution.py:538
  134.1 4.8 %collective-permute-start.18 = (bf16[196,256]{1,0:T(8,128)(2,1)S(1)}, bf16[196,256]{1,0:T(8,128)(2,1)S(1)}, u32[]{:S(2)}, u32[]{:S(2)}) collective-permute-start(bf16[196,256]{1,0:T(8,128)(2,1)S(1)} %add_convert_fusion.1), channel_id=1, source_target_pairs={{0,8},{1,9},{2,10},{3,11},{4,12},{5,13},{6,14},{7,15},{8,16},{9,17... | collective-permute-start | bytes 301064 | tf_op jit(solution)/shard_map/ppermute | solution.py:538
  135.8 5.0 %collective-permute-start.17 = (bf16[196,256]{1,0:T(8,128)(2,1)S(1)}, bf16[196,256]{1,0:T(8,128)(2,1)S(1)}, u32[]{:S(2)}, u32[]{:S(2)}) collective-permute-start(bf16[196,256]{1,0:T(8,128)(2,1)S(1)} %add_convert_fusion.1), channel_id=1, source_target_pairs={{0,16},{1,17},{2,18},{3,19},{4,20},{5,21},{6,22},{7,23},{8,24},{9,... | collective-permute-start | bytes 301064 | tf_op jit(solution)/shard_map/ppermute | solution.py:538
  136.2 4.8 %collective-permute-start.19 = (bf16[196,256]{1,0:T(8,128)(2,1)S(1)}, bf16[196,256]{1,0:T(8,128)(2,1)S(1)}, u32[]{:S(2)}, u32[]{:S(2)}) collective-permute-start(bf16[196,256]{1,0:T(8,128)(2,1)S(1)} %add_convert_fusion.1), channel_id=1, source_target_pairs={{0,24},{1,25},{2,26},{3,27},{4,28},{5,29},{6,30},{7,31},{8,0},{9,1... | collective-permute-start | bytes 301064 | tf_op jit(solution)/shard_map/ppermute | solution.py:538
  141.4 12.1 %collective-permute-start.22 = (bf16[304,256]{1,0:T(8,128)(2,1)S(1)}, bf16[304,256]{1,0:T(8,128)(2,1)S(1)}, u32[]{:S(2)}, u32[]{:S(2)}) collective-permute-start(bf16[304,256]{1,0:T(8,128)(2,1)S(1)} %pad_maximum_fusion.3), channel_id=1, source_target_pairs={{0,6},{1,7},{2,0},{3,1},{4,2},{5,3},{6,4},{7,5},{8,14},{9,15},{10,... | collective-permute-start | bytes 466952 | tf_op jit(solution)/shard_map/ppermute | solution.py:538
  141.5 12.0 %collective-permute-start.21 = (bf16[304,256]{1,0:T(8,128)(2,1)S(1)}, bf16[304,256]{1,0:T(8,128)(2,1)S(1)}, u32[]{:S(2)}, u32[]{:S(2)}) collective-permute-start(bf16[304,256]{1,0:T(8,128)(2,1)S(1)} %pad_maximum_fusion.3), channel_id=1, source_target_pairs={{0,2},{1,3},{2,4},{3,5},{4,6},{5,7},{6,0},{7,1},{8,10},{9,11},{10,... | collective-permute-start | bytes 466952 | tf_op jit(solution)/shard_map/ppermute | solution.py:538
  143.2 10.3 %collective-permute-start.20 = (bf16[304,256]{1,0:T(8,128)(2,1)S(1)}, bf16[304,256]{1,0:T(8,128)(2,1)S(1)}, u32[]{:S(2)}, u32[]{:S(2)}) collective-permute-start(bf16[304,256]{1,0:T(8,128)(2,1)S(1)} %pad_maximum_fusion.3), channel_id=1, source_target_pairs={{0,4},{1,5},{2,6},{3,7},{4,0},{5,1},{6,2},{7,3},{8,12},{9,13},{10,... | collective-permute-start | bytes 466952 | tf_op jit(solution)/shard_map/ppermute | solution.py:538
  145.0 14.7 %collective-permute-start.4 = (bf16[24,16,256]{2,1,0:T(8,128)(2,1)S(1)}, bf16[24,16,256]{2,1,0:T(8,128)(2,1)S(1)}, u32[]{:S(2)}, u32[]{:S(2)}) collective-permute-start(bf16[24,16,256]{2,1,0:T(8,128)(2,1)S(1)} %get-tuple-element.42), channel_id=1, source_target_pairs={{255,0},{0,1},{1,2},{2,3},{3,4},{4,5},{5,6},{6,7},{7,8},{8,9},{9,1... | collective-permute-start | bytes 589832 | tf_op jit(solution)/shard_map/ppermute | solution.py:520
  153.5 6.2 %collective-permute-start.5 = (bf16[24,16,256]{2,1,0:T(8,128)(2,1)S(1)}, bf16[24,16,256]{2,1,0:T(8,128)(2,1)S(1)}, u32[]{:S(2)}, u32[]{:S(2)}) collective-permute-start(bf16[24,16,256]{2,1,0:T(8,128)(2,1)S(1)} %get-tuple-element.43), channel_id=1, source_target_pairs={{1,0},{2,1},{3,2},{4,3},{5,4},{6,5},{7,6},{8,7},{9,8},{10,9},{11,1... | collective-permute-start | bytes 589832 | tf_op jit(solution)/shard_map/ppermute | solution.py:520
  153.7 15.3 %collective-permute-start.23 = (bf16[736,256]{1,0:T(8,128)(2,1)S(1)}, bf16[736,256]{1,0:T(8,128)(2,1)S(1)}, u32[]{:S(2)}, u32[]{:S(2)}) collective-permute-start(bf16[736,256]{1,0:T(8,128)(2,1)S(1)} %pad_maximum_fusion.2), channel_id=1, source_target_pairs={{0,1},{1,0},{2,3},{3,2},{4,5},{5,4},{6,7},{7,6},{8,9},{9,8},{10,11... | collective-permute-start | bytes 1130504 | tf_op jit(solution)/shard_map/ppermute | solution.py:538
  (9 other events, 54.7 us)
where the time goes:
time: 174 us; the launch traced here: 173 us
  Pallas kernels  90.9 us (52%)
  starting transfers between devices  52 us (30%)
  waiting for transfers between devices  17.1 us (10%)
  local copies, waits for them, and re-layouts  6.17 us (4%)
  other arithmetic  4.79 us (3%)
  between operations  1.95 us (1%)
    pallas_call x1, Pallas kernels, body(): call(front_kernel, [struct((14 * EP, SUB, CP), bf16), struct((14 * EW, SU...  34.8 us
    ppermute x18, starting transfers between devices, rotated(): return lax.ppermute(block, 'tiles', route)  29.9 us
    ppermute x6, starting transfers between devices, shifted(): lax.ppermute(block, 'tiles', [((i - distance) % count, i) for i in range(...  22.1 us
    pallas_call x1, Pallas kernels, body(): call(back_kernel, [struct((QROWS, SIDE, SUB, CP), f32), struct((24, SUB,...  18.1 us
    ppermute x18, waiting for transfers between devices, rotated(): return lax.ppermute(block, 'tiles', route)  15.3 us
    pallas_call x1, Pallas kernels, body(): call(taps_kernel, struct((49, CP), f32), [VMEM] * 4, [pltpu.VMEM((49, 8,...  14.6 us
    pallas_call x1, Pallas kernels, body(): call(final_kernel, struct(ocean_state.shape, bf16), [VMEM] * 5 + [SMEM],...  9.18 us
    pallas_call x1, Pallas kernels, body(): call(stem_kernel, [struct((QROWS, SIDE, SUB, CP), bf16), struct((QROWS, S...  6.8 us
  transfers between devices with their start and end apart: 24, of which 7 were waited for; matrix products, arithmetic and copies ran while one was open for 2% of the time, Pallas kernels for 27%

commit v1 on v0

--- a/solution.py
+++ b/solution.py
@@ -192,7 +192,7 @@
                 last_ref[r] = x[13:]
         return carry
 
-    lax.fori_loop(0, QROWS, visit, 0)
+    lax.fori_loop(0, QROWS, visit, 0, unroll=QROWS)
 
 
 def cot_kernel(cot_ref, wet_ref, out_ref):
@@ -208,7 +208,7 @@
             out_ref[r, 16 * h : 16 * h + 16] = dot(swap, x).astype(bf16).reshape(16, SUB, CW)
         return carry
 
-    lax.fori_loop(0, QROWS, visit, 0)
+    lax.fori_loop(0, QROWS, visit, 0, unroll=QROWS)
 
 
 def widen_kernel(
@@ -312,25 +312,18 @@
     ggain_ref[...] = jnp.zeros_like(ggain_ref)
     chosen_ref[...] = jnp.zeros_like(chosen_ref)
 
-    mixed_ref[:, :, :, :, :128] = jnp.zeros((QROWS, 16, 2, SUB, 128), f32)
-
-    def mix_rest(r):
+    def mix(r, carry):
+        pairs = conv_pairs(ext0_ref, r * EP, EP, 16, diag_ref, False)
+        for n in range(2):
+            half = pairs[:, 128 * n : 128 * n + 128]
+            mixed_ref[r, :, n, :, :128] = half.reshape(16, SUB, 128)
         for block in range(4):
             mixed_ref[r, 4 * block : 4 * block + 4, :, :, 128:] = conv_rest(
                 ext1_ref, r * EW + 8 * block, EW, 8, kf_ref, False
             ).reshape(4, 2, SUB, 128)
-
-    def mix(a, carry):
-        for r in (0, 4):
-            got = pair_term(ext0_ref, [(r + k + a) * EP for k in range(4)], 16, diag_ref, a, False)
-            for n in range(2):
-                half = got[:, 128 * n : 128 * n + 128].reshape(4, 16, SUB, 128)
-                mixed_ref[r : r + 4, :, n, :, :128] += half
-        mix_rest(a)
         return carry
 
-    lax.fori_loop(0, 7, mix, 0)
-    mix_rest(7)
+    lax.fori_loop(0, QROWS, mix, 0)
 
     def visit(r, carry):
         mixed = mixed_ref[r].reshape(512, CP)
@@ -369,7 +362,7 @@
         gm1_ref[pl.ds(r * GW + 6, SIDE)] = low_mixed[:, :, 128:]
         return carry
 
-    lax.fori_loop(0, QROWS, visit, 0)
+    lax.fori_loop(0, QROWS, visit, 0, unroll=2)
     rows_ref[...] = jnp.zeros_like(rows_ref)
     for t in range(3):
         total = jnp.zeros((EW, CP), f32)
@@ -512,7 +505,7 @@
                 ]
         return carry
 
-    lax.fori_loop(0, QROWS, visit, 0)
+    lax.fori_loop(0, QROWS, visit, 0, unroll=QROWS)
 
 
 def shifted(block, distance):
@@ -567,12 +560,25 @@
     return tree_sum([t.astype(f32) for t in terms])
 
 
-def sum_and_gather(block, count, level):
+def sum_kernel(*refs):
+    *terms, after_ref, out_ref = refs
+    rows = out_ref.shape[0]
+    out_ref[...] = tree_sum([t[:rows].astype(f32) for t in terms]).astype(bf16)
+
+
+def sum_and_gather(block, count, level, after):
     size = level[1]
     rows = block.shape[0] - count
     me = place_in(level)
     terms = [block] + [rotated(block, level, n) for n in range(1, size)]
-    total = tree_sum([t[:count].astype(f32) for t in terms]).astype(bf16)
+    if after is None:
+        total = tree_sum([t[:count].astype(f32) for t in terms]).astype(bf16)
+    else:
+        total = call(
+            sum_kernel,
+            struct((count, block.shape[1]), bf16),
+            [VMEM] * size + [pl.BlockSpec(memory_space=pl.ANY)],
+        )(*terms, after)
     out = jnp.zeros((rows * size,) + block.shape[1:], block.dtype)
     for n, term in enumerate(terms):
         out = lax.dynamic_update_slice_in_dim(out, term[count:], ((me - n) % size) * rows, 0)
@@ -707,7 +713,8 @@
     for level in plan[:2:-1]:
         pack = full_sum(pack, level).astype(bf16)
     for level in plan[2::-1]:
-        pack = sum_and_gather(pack, count, level)
+        after = grad_state if level == plan[:3][-1] else None
+        pack = sum_and_gather(pack, count, level, after)
     rest = pack[:count].astype(f32)
     big = pack[count:].astype(f32).reshape(2, 3, CW, CP)
     gup = jnp.concatenate([big[0, c] for c in range(3)], axis=1)

time: 174 us -> 164 us (0.943)
  Pallas kernels: 90.9 us -> 80.9 us
  starting transfers between devices: 52 us -> 49.9 us
    pallas_call x1, Pallas kernels: 9.18 us -> 5.53 us  [body(): call(final_kernel, struct(ocean_state.shape, bf16), [VMEM] * 5 + [SMEM],...]
    pallas_call x1, Pallas kernels: 34.8 us -> 32.1 us  [body(): call(front_kernel, [struct((14 * EP, SUB, CP), bf16), struct((14 * EW, SU...]
    pallas_call x1, Pallas kernels: 6.8 us -> 4.13 us  [body(): call(stem_kernel, [struct((QROWS, SIDE, SUB, CP), bf16), struct((QROWS, S...]
    ppermute x6, starting transfers between devices: 22.1 us -> 20 us  [shifted(): lax.ppermute(block, 'tiles', [((i - distance) % count, i) for i in range(...]
    unnamed x27 -> x29, local copies, waits for them, and re-layouts: 2.42 us -> 3.64 us
  transfers between devices with their start and end apart: 24 -> 24, of which waited for: 7 -> 5; matrix products, arithmetic and copies ran while one was open for 2% -> 2% of each run, Pallas kernels for 27% -> 26%
where the time goes in v1:
time: 164 us; the launch traced here: 163 us
  Pallas kernels  80.9 us (49%)
  starting transfers between devices  49.9 us (30%)
  waiting for transfers between devices  18.6 us (11%)
  local copies, waits for them, and re-layouts  7.47 us (5%)
  other arithmetic  4.74 us (3%)
  between operations  1.87 us (1%)
    pallas_call x1, Pallas kernels, body(): call(front_kernel, [struct((14 * EP, SUB, CP), bf16), struct((14 * EW, SU...  32.1 us
    ppermute x18, starting transfers between devices, rotated(): return lax.ppermute(block, 'tiles', route)  29.8 us
    ppermute x6, starting transfers between devices, shifted(): lax.ppermute(block, 'tiles', [((i - distance) % count, i) for i in range(...  20 us
    pallas_call x1, Pallas kernels, body(): call(back_kernel, [struct((QROWS, SIDE, SUB, CP), f32), struct((24, SUB,...  18.1 us
    ppermute x18, waiting for transfers between devices, rotated(): return lax.ppermute(block, 'tiles', route)  16.9 us
    pallas_call x1, Pallas kernels, body(): call(taps_kernel, struct((49, CP), f32), [VMEM] * 4, [pltpu.VMEM((49, 8,...  14.6 us
    pallas_call x1, Pallas kernels, body(): call(final_kernel, struct(ocean_state.shape, bf16), [VMEM] * 5 + [SMEM],...  5.53 us
    pallas_call x1, Pallas kernels, body(): call(stem_kernel, [struct((QROWS, SIDE, SUB, CP), bf16), struct((QROWS, S...  4.13 us
  transfers between devices with their start and end apart: 24, of which 5 were waited for; matrix products, arithmetic and copies ran while one was open for 2% of the time, Pallas kernels for 26%

profile of v1, /device:TPU:1, one launch (start us, length us, event | category | flops | bytes accessed | tf_op | source)
XLA Modules:
  0.0 163.5 jit_solution(12885340329486319652)
XLA Ops:
  1.7 4.1 %shard_map.145 = (bf16[8,32,16,256]{3,2,1,0:T(8,128)(2,1)}, bf16[8,32,16,95]{3,2,1,0:T(8,128)(2,1)S(1)}, bf16[8,3,16,95]{3,2,1,0:T(8,128)(2,1)S(1)}, bf16[8,3,16,95]{3,2,1,0:T(8,128)(2,1)S(1)}) custom-call(bf16[4,32,32,95]{3,2,1,0:T(8,128)(2,1)} %state_ref.1, bf16[95,256]{1,0:T(8,128)(2,1)S(1)} %pad.16.clone.w_ref.stem_w_ref), custom_call_target="tpu_custom_call" | custom-call | flops 5750000128 | bytes 5000000 | tf_op jit(solution)/shard_map/pallas_call | solution.py:612
  6.8 2.7 %collective-permute-start = (bf16[8,3,16,95]{3,2,1,0:T(8,128)(2,1)S(1)}, bf16[8,3,16,95]{3,2,1,0:T(8,128)(2,1)S(1)}, u32[]{:S(2)}, u32[]{:S(2)}) collective-permute-start(bf16[8,3,16,95]{3,2,1,0:T(8,128)(2,1)S(1)} %get-tuple-element.28), channel_id=1, source_target_pairs={{255,0},{0,1},{1,2},{2,3},{3,4},{4,5},{5,6},{6,7},{7,8},{8,9},{9,1... | collective-permute-start | bytes 218888 | tf_op jit(solution)/shard_map/ppermute | solution.py:513
  11.2 3.9 %shard_map.147.cot_ref = bf16[8,32,16,192]{3,2,1,0:T(8,128)(2,1)} custom-call(bf16[4,32,32,192]{3,2,1,0:T(8,128)(2,1)} %cot_ref.1, s32[1]{0:T(128)S(6)} %copy.38.wet_ref), custom_call_target="tpu_custom_call" | custom-call | flops 5750000128 | bytes 5000000 | tf_op jit(solution)/shard_map/pallas_call | solution.py:625
  15.1 1.3 broadcast_multiply_fusion.diag_ref
  16.5 2.5 %shard_map.146 = (bf16[24,16,95]{2,1,0:T(8,128)(2,1)S(1)}, bf16[24,16,95]{2,1,0:T(8,128)(2,1)S(1)}, bf16[24,16,256]{2,1,0:T(8,128)(2,1)S(1)}, bf16[24,16,256]{2,1,0:T(8,128)(2,1)S(1)}, bf16[128,256]{1,0:T(8,128)(2,1)S(1)}) custom-call(bf16[24,16,95]{2,1,0:T(8,128)(2,1)S(1)} %bitcast.36, bf16[24,16,95]{2,1,0:T(8,128)(2,1)S(1)} %bitcast.37, ...), custom_call_target="tpu_custom_call" | custom-call | flops 1150000000 | bytes 1000000 | tf_op jit(solution)/shard_map/pallas_call | solution.py:628
  19.0 6.6 %collective-permute-start.2 = (bf16[128,256]{1,0:T(8,128)(2,1)S(1)}, bf16[128,256]{1,0:T(8,128)(2,1)S(1)}, u32[]{:S(2)}, u32[]{:S(2)}) collective-permute-start(bf16[128,256]{1,0:T(8,128)(2,1)S(1)} %get-tuple-element.32), channel_id=1, source_target_pairs={{128,0},{129,1},{130,2},{131,3},{132,4},{133,5},{134,6},{135,7},{1... | collective-permute-start | bytes 196616 | tf_op jit(solution)/shard_map/ppermute | solution.py:513
  25.6 1.7 %collective-permute-done.2.partner_ref = bf16[128,256]{1,0:T(8,128)(2,1)S(1)} collective-permute-done((bf16[128,256]{1,0:T(8,128)(2,1)S(1)}, bf16[128,256]{1,0:T(8,128)(2,1)S(1)}, u32[]{:S(2)}, u32[]{:S(2)}) %collective-permute-start.2) | collective-permute-done | bytes 65568 | tf_op jit(solution)/shard_map/ppermute | solution.py:513
  27.3 32.1 %shard_map.148 = (bf16[266,16,256]{2,1,0:T(8,128)(2,1)}, bf16[532,16,128]{2,1,0:T(8,128)(2,1)}, bf16[176,16,256]{2,1,0:T(8,128)(2,1)}, bf16[352,16,128]{2,1,0:T(...) custom-call(bf16[8,32,16,256]{3,2,1,0:T(8,128)(2,1)} %get-tuple-elem, ...), custom_call_target="tpu_custom_call" | custom-call | flops 41400000512 | bytes 36000000 | tf_op jit(solution)/shard_map/pallas_call | solution.py:637
  60.9 8.3 %collective-permute-start.6 = (bf16[576,256]{1,0:T(8,128)(2,1)S(1)}, bf16[576,256]{1,0:T(8,128)(2,1)S(1)}, u32[]{:S(2)}, u32[]{:S(2)}) collective-permute-start(bf16[576,256]{1,0:T(8,128)(2,1)S(1)} %constant_dynamic-slice_fusion.6), channel_id=1, source_target_pairs={{0,1},{1,0},{2,3},{3,2},{4,5},{5,4},{6,7},{7,6},{8,9},{9,8},{10,11... | collective-permute-start | bytes 884744 | tf_op jit(solution)/shard_map/ppermute | solution.py:531
  69.2 4.2 %collective-permute-start.3 = (bf16[128,256]{1,0:T(8,128)(2,1)S(1)}, bf16[128,256]{1,0:T(8,128)(2,1)S(1)}, u32[]{:S(2)}, u32[]{:S(2)}) collective-permute-start(bf16[128,256]{1,0:T(8,128)(2,1)S(1)} %get-tuple-element.35), channel_id=1, source_target_pairs={{128,0},{129,1},{130,2},{131,3},{132,4},{133,5},{134,6},{135,7},{1... | collective-permute-start | bytes 196616 | tf_op jit(solution)/shard_map/ppermute | solution.py:513
  73.6 1.5 collective-permute-start.8
  75.1 14.6 %shard_map.149.after_ref = f32[49,256]{1,0:T(8,128)S(1)} custom-call(bf16[266,16,256]{2,1,0:T(8,128)(2,1)} %get-tuple-element.39.ext0_ref, bf16[532,16,128]{2,1,0:T(8,128)(2,1)} %get-tuple-element.40.ext1_ref, bf16[176,16,256]{2,1,0:T(8,128)(2,1)S(1)} %copy-done.5, bf16[352,16,128]{2,1,0:T(8,128)(2,1)} %get-tuple-element.34.gm1_ref), custom_call_target="tpu_custom_call" | custom-call | flops 17250000896 | bytes 15000000 | tf_op jit(solution)/shard_map/pallas_call | solution.py:663
  92.3 18.1 %shard_map.150 = (f32[8,32,16,256]{3,2,1,0:T(8,128)}, bf16[24,16,256]{2,1,0:T(8,128)(2,1)S(1)}, bf16[24,16,256]{2,1,0:T(8,128)(2,1)S(1)}, f32[95,256]{1,0:T(8,128)S(1)}) custom-call(bf16[176,16,256]{2,1,0:T(8,128)(2,1)} %get-tuple-element.33.gm0_ref, bf16[352,16,128]{2,1,0:T(8,128)(2,1)} %get-tuple-element.34.gm1_ref, ...), custom_call_target="tpu_custom_call" | custom-call | flops 23000000512 | bytes 20000000 | tf_op jit(solution)/shard_map/pallas_call | solution.py:670
  110.8 1.3 collective-permute-start.13
  112.1 7.0 %collective-permute-done.13 = bf16[196,256]{1,0:T(8,128)(2,1)S(1)} collective-permute-done((bf16[196,256]{1,0:T(8,128)(2,1)S(1)}, bf16[196,256]{1,0:T(8,128)(2,1)S(1)}, u32[]{:S(2)}, u32[]{:S(2)}) %collective-permute-start.13) | collective-permute-done | bytes 100384 | tf_op jit(solution)/shard_map/ppermute | solution.py:531
  121.8 6.0 %collective-permute-start.4 = (bf16[24,16,256]{2,1,0:T(8,128)(2,1)S(1)}, bf16[24,16,256]{2,1,0:T(8,128)(2,1)S(1)}, u32[]{:S(2)}, u32[]{:S(2)}) collective-permute-start(bf16[24,16,256]{2,1,0:T(8,128)(2,1)S(1)} %get-tuple-element.42), channel_id=1, source_target_pairs={{255,0},{0,1},{1,2},{2,3},{3,4},{4,5},{5,6},{6,7},{7,8},{8,9},{9,1... | collective-permute-start | bytes 589832 | tf_op jit(solution)/shard_map/ppermute | solution.py:513
  127.9 3.1 %collective-permute-start.17 = (bf16[196,256]{1,0:T(8,128)(2,1)S(1)}, bf16[196,256]{1,0:T(8,128)(2,1)S(1)}, u32[]{:S(2)}, u32[]{:S(2)}) collective-permute-start(bf16[196,256]{1,0:T(8,128)(2,1)S(1)} %add_convert_fusion.1.refs_0_), channel_id=1, source_target_pairs={{0,8},{1,9},{2,10},{3,11},{4,12},{5,13},{6,14},{7,15},{8,16},{9,17... | collective-permute-start | bytes 301064 | tf_op jit(solution)/shard_map/ppermute | solution.py:531
  131.0 1.9 %collective-permute-start.18 = (bf16[196,256]{1,0:T(8,128)(2,1)S(1)}, bf16[196,256]{1,0:T(8,128)(2,1)S(1)}, u32[]{:S(2)}, u32[]{:S(2)}) collective-permute-start(bf16[196,256]{1,0:T(8,128)(2,1)S(1)} %add_convert_fusion.1.refs_0_), channel_id=1, source_target_pairs={{0,16},{1,17},{2,18},{3,19},{4,20},{5,21},{6,22},{7,23},{8,24},{9,... | collective-permute-start | bytes 301064 | tf_op jit(solution)/shard_map/ppermute | solution.py:531
  132.9 2.0 %collective-permute-start.19 = (bf16[196,256]{1,0:T(8,128)(2,1)S(1)}, bf16[196,256]{1,0:T(8,128)(2,1)S(1)}, u32[]{:S(2)}, u32[]{:S(2)}) collective-permute-start(bf16[196,256]{1,0:T(8,128)(2,1)S(1)} %add_convert_fusion.1.refs_0_), channel_id=1, source_target_pairs={{0,24},{1,25},{2,26},{3,27},{4,28},{5,29},{6,30},{7,31},{8,0},{9,1... | collective-permute-start | bytes 301064 | tf_op jit(solution)/shard_map/ppermute | solution.py:531
  134.9 5.5 %shard_map.151.refs_4_ = bf16[4,32,32,95]{3,2,1,0:T(8,128)(2,1)} custom-call(f32[8,32,16,256]{3,2,1,0:T(8,128)} %get-tuple-element.41.mid_ref, bf16[8,32,16,192]{3,2,1,0:T(8,128)(2,1)} %shard_map.147.cot_ref, bf16[24,16,256]{2,1,0:T(8,128)(2,1)S(1)} %collective-permute-done.4.w_ref, bf16[24,16,256]{2,1,0:T(8,128)(2,1)S(1)} %collective-permute-done.5.e_ref, ...), custom_call_target="tpu_custom_call" | custom-call | flops 9200000000 | bytes 8000000 | tf_op jit(solution)/shard_map/pallas_call | solution.py:701
  142.9 4.2 %collective-permute-start.22 = (bf16[304,256]{1,0:T(8,128)(2,1)S(1)}, bf16[304,256]{1,0:T(8,128)(2,1)S(1)}, u32[]{:S(2)}, u32[]{:S(2)}) collective-permute-start(bf16[304,256]{1,0:T(8,128)(2,1)S(1)} %pad_maximum_fusion.3), channel_id=1, source_target_pairs={{0,6},{1,7},{2,0},{3,1},{4,2},{5,3},{6,4},{7,5},{8,14},{9,15},{10,... | collective-permute-start | bytes 466952 | tf_op jit(solution)/shard_map/ppermute | solution.py:531
  147.1 1.3 collective-permute-start.20
  148.4 1.8 %collective-permute-done.22 = bf16[304,256]{1,0:T(8,128)(2,1)S(1)} collective-permute-done((bf16[304,256]{1,0:T(8,128)(2,1)S(1)}, bf16[304,256]{1,0:T(8,128)(2,1)S(1)}, u32[]{:S(2)}, u32[]{:S(2)}) %collective-permute-start.22) | collective-permute-done | bytes 155680 | tf_op jit(solution)/shard_map/ppermute | solution.py:531
  150.2 6.9 %collective-permute-done.21 = bf16[304,256]{1,0:T(8,128)(2,1)S(1)} collective-permute-done((bf16[304,256]{1,0:T(8,128)(2,1)S(1)}, bf16[304,256]{1,0:T(8,128)(2,1)S(1)}, u32[]{:S(2)}, u32[]{:S(2)}) %collective-permute-start.21) | collective-permute-done | bytes 155680 | tf_op jit(solution)/shard_map/ppermute | solution.py:531
  (118 shorter events, 19.1 us)
Async XLA Ops:
  6.8 9.6 %collective-permute-start = (bf16[8,3,16,95]{3,2,1,0:T(8,128)(2,1)S(1)}, bf16[8,3,16,95]{3,2,1,0:T(8,128)(2,1)S(1)}, u32[]{:S(2)}, u32[]{:S(2)}) collective-permute-start(bf16[8,3,16,95]{3,2,1,0:T(8,128)(2,1)S(1)} %get-tuple-element.28), channel_id=1, source_target_pairs={{255,0},{0,1},{1,2},{2,3},{3,4},{4,5},{5,6},{6,7},{7,8},{8,9},{9,1... | collective-permute-start | bytes 218888 | tf_op jit(solution)/shard_map/ppermute | solution.py:513
  9.5 6.9 %collective-permute-start.1 = (bf16[8,3,16,95]{3,2,1,0:T(8,128)(2,1)S(1)}, bf16[8,3,16,95]{3,2,1,0:T(8,128)(2,1)S(1)}, u32[]{:S(2)}, u32[]{:S(2)}) collective-permute-start(bf16[8,3,16,95]{3,2,1,0:T(8,128)(2,1)S(1)} %get-tuple-element.29), channel_id=1, source_target_pairs={{1,0},{2,1},{3,2},{4,3},{5,4},{6,5},{7,6},{8,7},{9,8},{10,9},{11,1... | collective-permute-start | bytes 218888 | tf_op jit(solution)/shard_map/ppermute | solution.py:513
  19.0 8.3 %collective-permute-start.2 = (bf16[128,256]{1,0:T(8,128)(2,1)S(1)}, bf16[128,256]{1,0:T(8,128)(2,1)S(1)}, u32[]{:S(2)}, u32[]{:S(2)}) collective-permute-start(bf16[128,256]{1,0:T(8,128)(2,1)S(1)} %get-tuple-element.32), channel_id=1, source_target_pairs={{128,0},{129,1},{130,2},{131,3},{132,4},{133,5},{134,6},{135,7},{1... | collective-permute-start | bytes 196616 | tf_op jit(solution)/shard_map/ppermute | solution.py:513
  60.9 12.5 %collective-permute-start.6 = (bf16[576,256]{1,0:T(8,128)(2,1)S(1)}, bf16[576,256]{1,0:T(8,128)(2,1)S(1)}, u32[]{:S(2)}, u32[]{:S(2)}) collective-permute-start(bf16[576,256]{1,0:T(8,128)(2,1)S(1)} %constant_dynamic-slice_fusion.6), channel_id=1, source_target_pairs={{0,1},{1,0},{2,3},{3,2},{4,5},{5,4},{6,7},{7,6},{8,9},{9,8},{10,11... | collective-permute-start | bytes 884744 | tf_op jit(solution)/shard_map/ppermute | solution.py:531
  69.2 23.1 %collective-permute-start.3 = (bf16[128,256]{1,0:T(8,128)(2,1)S(1)}, bf16[128,256]{1,0:T(8,128)(2,1)S(1)}, u32[]{:S(2)}, u32[]{:S(2)}) collective-permute-start(bf16[128,256]{1,0:T(8,128)(2,1)S(1)} %get-tuple-element.35), channel_id=1, source_target_pairs={{128,0},{129,1},{130,2},{131,3},{132,4},{133,5},{134,6},{135,7},{1... | collective-permute-start | bytes 196616 | tf_op jit(solution)/shard_map/ppermute | solution.py:513
  73.5 16.2 %collective-permute-start.9 = (bf16[144,256]{1,0:T(8,128)(2,1)S(1)}, bf16[144,256]{1,0:T(8,128)(2,1)S(1)}, u32[]{:S(2)}, u32[]{:S(2)}) collective-permute-start(bf16[144,256]{1,0:T(8,128)(2,1)S(1)} %get-tuple-element.55), channel_id=1, source_target_pairs={{0,6},{1,7},{2,0},{3,1},{4,2},{5,3},{6,4},{7,5},{8,14},{9,15},{10,... | collective-permute-start | bytes 221192 | tf_op jit(solution)/shard_map/ppermute | solution.py:531
  73.6 16.1 %collective-permute-start.8 = (bf16[144,256]{1,0:T(8,128)(2,1)S(1)}, bf16[144,256]{1,0:T(8,128)(2,1)S(1)}, u32[]{:S(2)}, u32[]{:S(2)}) collective-permute-start(bf16[144,256]{1,0:T(8,128)(2,1)S(1)} %get-tuple-element.56), channel_id=1, source_target_pairs={{0,2},{1,3},{2,4},{3,5},{4,6},{5,7},{6,0},{7,1},{8,10},{9,11},{10,... | collective-permute-start | bytes 221192 | tf_op jit(solution)/shard_map/ppermute | solution.py:531
  75.1 14.7 %collective-permute-start.7 = (bf16[144,256]{1,0:T(8,128)(2,1)S(1)}, bf16[144,256]{1,0:T(8,128)(2,1)S(1)}, u32[]{:S(2)}, u32[]{:S(2)}) collective-permute-start(bf16[144,256]{1,0:T(8,128)(2,1)S(1)} %get-tuple-element.54), channel_id=1, source_target_pairs={{0,4},{1,5},{2,6},{3,7},{4,0},{5,1},{6,2},{7,3},{8,12},{9,13},{10,... | collective-permute-start | bytes 221192 | tf_op jit(solution)/shard_map/ppermute | solution.py:531
  89.9 20.6 %collective-permute-start.12 = (bf16[36,256]{1,0:T(8,128)(2,1)S(1)}, bf16[36,256]{1,0:T(8,128)(2,1)S(1)}, u32[]{:S(2)}, u32[]{:S(2)}) collective-permute-start(bf16[36,256]{1,0:T(8,128)(2,1)S(1)} %get-tuple-element.58), channel_id=1, source_target_pairs={{0,24},{1,25},{2,26},{3,27},{4,28},{5,29},{6,30},{7,31},{8,0},{9,1... | collective-permute-start | bytes 55304 | tf_op jit(solution)/shard_map/ppermute | solution.py:531
  91.0 19.4 %collective-permute-start.11 = (bf16[36,256]{1,0:T(8,128)(2,1)S(1)}, bf16[36,256]{1,0:T(8,128)(2,1)S(1)}, u32[]{:S(2)}, u32[]{:S(2)}) collective-permute-start(bf16[36,256]{1,0:T(8,128)(2,1)S(1)} %get-tuple-element.59), channel_id=1, source_target_pairs={{0,8},{1,9},{2,10},{3,11},{4,12},{5,13},{6,14},{7,15},{8,16},{9,17... | collective-permute-start | bytes 55304 | tf_op jit(solution)/shard_map/ppermute | solution.py:531
  91.4 19.0 %collective-permute-start.10 = (bf16[36,256]{1,0:T(8,128)(2,1)S(1)}, bf16[36,256]{1,0:T(8,128)(2,1)S(1)}, u32[]{:S(2)}, u32[]{:S(2)}) collective-permute-start(bf16[36,256]{1,0:T(8,128)(2,1)S(1)} %get-tuple-element.57), channel_id=1, source_target_pairs={{0,16},{1,17},{2,18},{3,19},{4,20},{5,21},{6,22},{7,23},{8,24},{9,... | collective-permute-start | bytes 55304 | tf_op jit(solution)/shard_map/ppermute | solution.py:531
  110.8 8.3 %collective-permute-start.13 = (bf16[196,256]{1,0:T(8,128)(2,1)S(1)}, bf16[196,256]{1,0:T(8,128)(2,1)S(1)}, u32[]{:S(2)}, u32[]{:S(2)}) collective-permute-start(bf16[196,256]{1,0:T(8,128)(2,1)S(1)} %concatenate.23), channel_id=1, source_target_pairs={{0,128},{1,129},{2,130},{3,131},{4,132},{5,133},{6,134},{7,135},{8... | collective-permute-start | bytes 301064 | tf_op jit(solution)/shard_map/ppermute | solution.py:531
  119.1 8.7 %collective-permute-start.16 = (bf16[196,256]{1,0:T(8,128)(2,1)S(1)}, bf16[196,256]{1,0:T(8,128)(2,1)S(1)}, u32[]{:S(2)}, u32[]{:S(2)}) collective-permute-start(bf16[196,256]{1,0:T(8,128)(2,1)S(1)} %add_convert_fusion.2), channel_id=1, source_target_pairs={{0,96},{1,97},{2,98},{3,99},{4,100},{5,101},{6,102},{7,103},{8,104... | collective-permute-start | bytes 301064 | tf_op jit(solution)/shard_map/ppermute | solution.py:531
  119.5 8.3 %collective-permute-start.15 = (bf16[196,256]{1,0:T(8,128)(2,1)S(1)}, bf16[196,256]{1,0:T(8,128)(2,1)S(1)}, u32[]{:S(2)}, u32[]{:S(2)}) collective-permute-start(bf16[196,256]{1,0:T(8,128)(2,1)S(1)} %add_convert_fusion.2), channel_id=1, source_target_pairs={{0,32},{1,33},{2,34},{3,35},{4,36},{5,37},{6,38},{7,39},{8,40},{9,... | collective-permute-start | bytes 301064 | tf_op jit(solution)/shard_map/ppermute | solution.py:531
  120.7 7.1 %collective-permute-start.14 = (bf16[196,256]{1,0:T(8,128)(2,1)S(1)}, bf16[196,256]{1,0:T(8,128)(2,1)S(1)}, u32[]{:S(2)}, u32[]{:S(2)}) collective-permute-start(bf16[196,256]{1,0:T(8,128)(2,1)S(1)} %add_convert_fusion.2), channel_id=1, source_target_pairs={{0,64},{1,65},{2,66},{3,67},{4,68},{5,69},{6,70},{7,71},{8,72},{9,... | collective-permute-start | bytes 301064 | tf_op jit(solution)/shard_map/ppermute | solution.py:531
  121.8 13.1 %collective-permute-start.4 = (bf16[24,16,256]{2,1,0:T(8,128)(2,1)S(1)}, bf16[24,16,256]{2,1,0:T(8,128)(2,1)S(1)}, u32[]{:S(2)}, u32[]{:S(2)}) collective-permute-start(bf16[24,16,256]{2,1,0:T(8,128)(2,1)S(1)} %get-tuple-element.42), channel_id=1, source_target_pairs={{255,0},{0,1},{1,2},{2,3},{3,4},{4,5},{5,6},{6,7},{7,8},{8,9},{9,1... | collective-permute-start | bytes 589832 | tf_op jit(solution)/shard_map/ppermute | solution.py:513
  127.8 7.1 %collective-permute-start.5 = (bf16[24,16,256]{2,1,0:T(8,128)(2,1)S(1)}, bf16[24,16,256]{2,1,0:T(8,128)(2,1)S(1)}, u32[]{:S(2)}, u32[]{:S(2)}) collective-permute-start(bf16[24,16,256]{2,1,0:T(8,128)(2,1)S(1)} %get-tuple-element.43), channel_id=1, source_target_pairs={{1,0},{2,1},{3,2},{4,3},{5,4},{6,5},{7,6},{8,7},{9,8},{10,9},{11,1... | collective-permute-start | bytes 589832 | tf_op jit(solution)/shard_map/ppermute | solution.py:513
  127.9 12.8 %collective-permute-start.17 = (bf16[196,256]{1,0:T(8,128)(2,1)S(1)}, bf16[196,256]{1,0:T(8,128)(2,1)S(1)}, u32[]{:S(2)}, u32[]{:S(2)}) collective-permute-start(bf16[196,256]{1,0:T(8,128)(2,1)S(1)} %add_convert_fusion.1.refs_0_), channel_id=1, source_target_pairs={{0,8},{1,9},{2,10},{3,11},{4,12},{5,13},{6,14},{7,15},{8,16},{9,17... | collective-permute-start | bytes 301064 | tf_op jit(solution)/shard_map/ppermute | solution.py:531
  131.0 10.0 %collective-permute-start.18 = (bf16[196,256]{1,0:T(8,128)(2,1)S(1)}, bf16[196,256]{1,0:T(8,128)(2,1)S(1)}, u32[]{:S(2)}, u32[]{:S(2)}) collective-permute-start(bf16[196,256]{1,0:T(8,128)(2,1)S(1)} %add_convert_fusion.1.refs_0_), channel_id=1, source_target_pairs={{0,16},{1,17},{2,18},{3,19},{4,20},{5,21},{6,22},{7,23},{8,24},{9,... | collective-permute-start | bytes 301064 | tf_op jit(solution)/shard_map/ppermute | solution.py:531
  132.9 8.4 %collective-permute-start.19 = (bf16[196,256]{1,0:T(8,128)(2,1)S(1)}, bf16[196,256]{1,0:T(8,128)(2,1)S(1)}, u32[]{:S(2)}, u32[]{:S(2)}) collective-permute-start(bf16[196,256]{1,0:T(8,128)(2,1)S(1)} %add_convert_fusion.1.refs_0_), channel_id=1, source_target_pairs={{0,24},{1,25},{2,26},{3,27},{4,28},{5,29},{6,30},{7,31},{8,0},{9,1... | collective-permute-start | bytes 301064 | tf_op jit(solution)/shard_map/ppermute | solution.py:531
  142.9 7.3 %collective-permute-start.22 = (bf16[304,256]{1,0:T(8,128)(2,1)S(1)}, bf16[304,256]{1,0:T(8,128)(2,1)S(1)}, u32[]{:S(2)}, u32[]{:S(2)}) collective-permute-start(bf16[304,256]{1,0:T(8,128)(2,1)S(1)} %pad_maximum_fusion.3), channel_id=1, source_target_pairs={{0,6},{1,7},{2,0},{3,1},{4,2},{5,3},{6,4},{7,5},{8,14},{9,15},{10,... | collective-permute-start | bytes 466952 | tf_op jit(solution)/shard_map/ppermute | solution.py:531
  147.1 10.0 %collective-permute-start.21 = (bf16[304,256]{1,0:T(8,128)(2,1)S(1)}, bf16[304,256]{1,0:T(8,128)(2,1)S(1)}, u32[]{:S(2)}, u32[]{:S(2)}) collective-permute-start(bf16[304,256]{1,0:T(8,128)(2,1)S(1)} %pad_maximum_fusion.3), channel_id=1, source_target_pairs={{0,2},{1,3},{2,4},{3,5},{4,6},{5,7},{6,0},{7,1},{8,10},{9,11},{10,... | collective-permute-start | bytes 466952 | tf_op jit(solution)/shard_map/ppermute | solution.py:531
  147.1 10.0 %collective-permute-start.20 = (bf16[304,256]{1,0:T(8,128)(2,1)S(1)}, bf16[304,256]{1,0:T(8,128)(2,1)S(1)}, u32[]{:S(2)}, u32[]{:S(2)}) collective-permute-start(bf16[304,256]{1,0:T(8,128)(2,1)S(1)} %pad_maximum_fusion.3), channel_id=1, source_target_pairs={{0,4},{1,5},{2,6},{3,7},{4,0},{5,1},{6,2},{7,3},{8,12},{9,13},{10,... | collective-permute-start | bytes 466952 | tf_op jit(solution)/shard_map/ppermute | solution.py:531
  157.2 2.4 %collective-permute-start.23 = (bf16[736,256]{1,0:T(8,128)(2,1)S(1)}, bf16[736,256]{1,0:T(8,128)(2,1)S(1)}, u32[]{:S(2)}, u32[]{:S(2)}) collective-permute-start(bf16[736,256]{1,0:T(8,128)(2,1)S(1)} %pad_maximum_fusion.2), channel_id=1, source_target_pairs={{0,1},{1,0},{2,3},{3,2},{4,5},{5,4},{6,7},{7,6},{8,9},{9,8},{10,11... | collective-permute-start | bytes 1130504 | tf_op jit(solution)/shard_map/ppermute | solution.py:531
  (10 other events, 50.8 us)
